TPU v7x, 256 devices: a whole 4x4x8 slice. The times are simulated.
256 devices in a mesh: row: 8 (over z), col: 32 (over x, y, core).
Axes of the slice: x: 4, y: 4, z: 8, core: 2. Of those that a mesh axis runs over, the one named last changes fastest.
Arguments:
- schur_blocks: bfloat16 [8, 32, 2048, 2048], P('row', 'col'), as said below
- rigid_modes: float32 [8, 32, 6, 2048], P('row', 'col'), may hold values from -0.125 to 0.125
- floating: int32 [8, 32], P('row', 'col'), may hold values 0 or 1
- block_order: int32 [8, 32, 16], P('row', 'col'), may hold values from 0 to 15, each once within a row
- coarse_inverse: float32 [6, 8, 32, 6, 8, 32], P(None, 'row', None, None, None, 'col'), may hold values from -4 to 4
- right_side: float32 [8, 32, 2, 128, 512], P('row', 'col')
Outputs:
- multipliers: float32 [8, 32, 2, 128, 512], P('row', 'col')
- residual: float32 [8, 32, 2, 128, 512], P('row', 'col')
Inputs may be any that keep to these rules, and one draw needn't show every extreme that they name: `schur_blocks`: each subdomain's matrix is symmetric. `block_order`: each subdomain's 16 entries name every block of its face order once.
All inputs are finite; a program needn't handle non-finite values. No bound on the sum of `floating` on one device may be relied on, other than what follows from the above.
Results may differ from a plain program's by a relative error of at most 0.0003.
Values sent between devices are 32-bit elements; how exact they have to be, the bound alone decides.
No kernel may reach another device: no remote copies, remote signals or barrier semaphores. Data moves between devices by JAX's collectives and lax.ppermute only.
A program may use at most 128 MiB of HBM per device.

v0:
```python
import functools

import jax
import jax.numpy as jnp
from jax import lax
from jax.experimental import pallas as pl
from jax.experimental.pallas import tpu as pltpu
from jax.sharding import PartitionSpec as P

M = 512
NS = 2048
BLK = 128
NB = 16
K = 128
ROWS = 8
COLS = 32
MODES = 6
ITERS = 3
SLOT = 8
SLOTS = 5
PAY = 48
TERMS = ((0, 0), (0, 1), (1, 0), (1, 1), (0, 2), (2, 0))
TALL = 512
CHIPS = 16

f32 = jnp.float32
bf16 = jnp.bfloat16
VM = pl.BlockSpec(memory_space=pltpu.VMEM)
SM = pl.BlockSpec(memory_space=pltpu.SMEM)
LIMIT = pltpu.CompilerParams(vmem_limit_bytes=40 * 1024 * 1024)


def cyclic(value, axis, steps):
    count = lax.axis_size(axis)
    return lax.ppermute(value, axis, [(s, (s + steps) % count) for s in range(count)])


def shifted(value, axis, steps):
    count = lax.axis_size(axis)
    initial, last = (max(0, -steps), min(count, count - steps))
    return lax.ppermute(value, axis, [(s, s + steps) for s in range(initial, last)])


def swapped(value, partner):
    return lax.ppermute(value, "col", [(s, partner(s)) for s in range(COLS)])


def parts_of(value, count):
    pieces = []
    for _ in range(count):
        piece = value.astype(bf16)
        pieces.append(piece)
        value = value - piece.astype(f32)
    return pieces


def pay_from(bgt, halves):
    d = jnp.dot(bgt[...], halves[...], preferred_element_type=f32)
    return d[0:PAY, :K] + d[0:PAY, K:] + d[PAY : 2 * PAY, :K] + d[PAY : 2 * PAY, K:] + d[2 * PAY :, :K]


def hand_in(value, pay):
    for index in range(ROWS):
        pay[index] = value


def start_kernel(masks, own, side, from_n, from_w, local, pay, full, halves):
    full[...] = jnp.zeros_like(full)
    full[0:MODES, 0:M] = own[:, 0:M] * masks[0]
    full[0:MODES, M : 2 * M] = own[:, M : 2 * M]
    full[0:MODES, 2 * M : 3 * M] = own[:, 2 * M : 3 * M] * masks[2]
    full[0:MODES, 3 * M :] = own[:, 3 * M :]
    for face in range(4):
        for block in range(M // BLK):
            inside = slice(BLK * block, BLK * (block + 1))
            rows = slice(M * face + BLK * block, M * face + BLK * (block + 1))
            if face == 0:
                turned = from_n[:, inside].T * -masks[0]
            elif face == 2:
                turned = from_w[:, inside].T * -masks[2]
            else:
                turned = side[face // 2, :, inside].T
            local[rows, :] = turned
            high, low = parts_of(turned, 2)
            halves[rows, :K] = high
            halves[rows, K:] = low
    pieces = jnp.concatenate(parts_of(full[...], 3), axis=0)
    d = jnp.dot(pieces, halves[...], preferred_element_type=f32)
    value = d[0:16, :K] + d[0:16, K:] + d[16:32, :K] + d[16:32, K:] + d[32:48, :K]
    pay[...] = jnp.zeros_like(pay)
    for index in range(ROWS):
        pay[index, 0:SLOT, :] = value[0:SLOT]


def modes_kernel(masks, own, near_n, near_s, near_w, near_e, bgt, full):
    full[...] = jnp.zeros_like(full)
    full[0:MODES, 0:M] = own[:, 0:M] * masks[0]
    full[0:MODES, M : 2 * M] = own[:, M : 2 * M]
    full[0:MODES, 2 * M : 3 * M] = own[:, 2 * M : 3 * M] * masks[2]
    full[0:MODES, 3 * M :] = own[:, 3 * M :]
    for slot, near in enumerate((near_n, near_s, near_w, near_e)):
        full[SLOT * (slot + 1) : SLOT * (slot + 1) + MODES, M * slot : M * (slot + 1)] = -near[...]
    for index, piece in enumerate(parts_of(full[...], 3)):
        bgt[PAY * index : PAY * (index + 1), :] = piece


def table_kernel(core, west, mine, east, far, parts, full):
    first = core[0] == 0
    left = lax.broadcasted_iota(jnp.int32, (SLOT, BLK), 1) < SLOT * ROWS
    for target in range(CHIPS):
        at = 2 * target + core[0]
        picks = ((0, at), (1, at), (2, at), (0, jnp.maximum(at - 1, 0)), (0, jnp.minimum(at + 1, COLS - 1)))
        for slot, (line, column) in enumerate(picks):
            w, m, e, f = west[line, column], mine[line, column], east[line, column], far[line, column]
            inner = jnp.where(left, jnp.where(first, w, f), jnp.where(first, m, w))
            outer = jnp.where(left, jnp.where(first, e, m), jnp.where(first, f, e))
            rows = slice((target * SLOTS + slot) * SLOT, (target * SLOTS + slot + 1) * SLOT)
            full[rows, :K] = inner
            full[rows, K:] = outer
    for index, piece in enumerate(parts_of(full[...], 3)):
        parts[index] = piece


def coarse_kernel(core, parts, own, other, out, entries):
    first = core[0] == 0

    def tile(which, line, slot):
        here = slice(SLOT * slot, SLOT * (slot + 1))
        a, b = own[line, here, :], other[line, here, :]
        return jnp.where(first, a, b) if which == 0 else jnp.where(first, b, a)

    total = jnp.zeros((SLOT, K), f32)
    for line in range(ROWS):
        for which in range(2):
            value = tile(which, line, 0)
            if line > 0:
                value = value + tile(which, line - 1, 2)
            if line < ROWS - 1:
                value = value + tile(which, line + 1, 1)
            value = value + tile(1 - which, line, 3 + which)
            at = SLOT * (ROWS * (which + 1) + line)
            entries[at : at + SLOT, :] = value
        entries[SLOT * line : SLOT * (line + 1), :] = tile(0, line, 3)
        at = SLOT * (ROWS * 3 + line)
        entries[at : at + SLOT, :] = tile(1, line, 4)
        total = total + own[line, SLOT * SLOTS :, :] + other[line, SLOT * SLOTS :, :]
    z1, z2, z3 = parts_of(entries[...], 3)
    both = jnp.concatenate([z1, z2], axis=1)
    d = jnp.dot(parts[0], both, preferred_element_type=f32)
    e = jnp.dot(parts[1], both, preferred_element_type=f32)
    value = jnp.dot(parts[0], z3, preferred_element_type=f32) + jnp.dot(parts[2], z1, preferred_element_type=f32)
    value = value + e[:, K:] + e[:, :K] + d[:, K:] + d[:, :K]
    for target in range(CHIPS):
        out[target] = value[SLOTS * SLOT * target : SLOTS * SLOT * (target + 1)]
        out[target, 6:8, :] = total[0:2]
        out[target, 14:15, :] = total[2:3]


def spread_kernel(bgt, bgc, turned):
    for index, (left, _) in enumerate(TERMS):
        rows = bgt[PAY * left : PAY * (left + 1), :].astype(f32)
        turned[40 * index : 40 * (index + 1), :] = rows[0:40]
    turned[240:256, :] = jnp.zeros((16, NS), f32)
    for block in range(NB):
        for half in range(2):
            piece = turned[BLK * half : BLK * (half + 1), BLK * block : BLK * (block + 1)].T
            bgc[BLK * block : BLK * (block + 1), BLK * half : BLK * (half + 1)] = piece.astype(bf16)


def take_values(came, stack):
    value = came[0]
    for index in range(1, CHIPS):
        value = value + came[index]
    spare = lax.broadcasted_iota(jnp.int32, (SLOT * SLOTS, K), 0) % SLOT >= MODES
    pieces = parts_of(jnp.where(spare, 0.0, value), 3)
    for index, (_, right) in enumerate(TERMS):
        stack[40 * index : 40 * (index + 1), :] = pieces[right].astype(f32)
    stack[240:256, :] = jnp.zeros((16, K), f32)
    return stack[...].astype(bf16), (value[6:7], value[7:8], value[14:15])


def schur_product(order, matrix, vector, halves, product, copies):
    for block in range(NB):
        at = pl.multiple_of(order[block] * BLK, BLK)
        high, low = parts_of(vector[pl.ds(at, BLK), :], 2)
        halves[BLK * block : BLK * (block + 1), :K] = high
        halves[BLK * block : BLK * (block + 1), K:] = low

    def tall(step):
        rows = matrix[pl.ds(pl.multiple_of(step * TALL, TALL), TALL), :]
        both = jnp.dot(rows, halves[...], preferred_element_type=f32)
        both = both[:, :K] + both[:, K:]
        for piece in range(TALL // BLK):
            at = pl.multiple_of(order[step * (TALL // BLK) + piece] * BLK, BLK)
            product[pl.ds(at, BLK), :] = both[BLK * piece : BLK * (piece + 1)]

    if copies:
        for step, copy in enumerate(copies):
            copy.wait()
            tall(step)
    else:
        pl.loop(0, NS // TALL)(tall)


def finish(order, matrix, bgt, residual, image, faces, pay, halves, product, copies=()):
    schur_product(order, matrix, residual, halves, product, copies)
    norm = jnp.zeros((1, K), f32)
    energy = jnp.zeros((1, K), f32)
    cross = jnp.zeros((1, K), f32)
    for face in range(4):
        for block in range(M // BLK):
            inside = slice(BLK * block, BLK * (block + 1))
            rows = slice(M * face + BLK * block, M * face + BLK * (block + 1))
            r = residual[rows, :]
            y = product[rows, :]
            faces[face][inside, :] = y
            high, low = parts_of(y, 2)
            halves[rows, :K] = high
            halves[rows, K:] = low
            energy = energy + jnp.sum(r * y, axis=0, keepdims=True)
            if face % 2:
                norm = norm + jnp.sum(r * r, axis=0, keepdims=True)
            if image is not None:
                cross = cross + jnp.sum(r * image[rows, :], axis=0, keepdims=True)
    hand_in(pay_from(bgt, halves), pay)
    for index in range(ROWS):
        pay[index, 40:41, :] = norm
        pay[index, 41:42, :] = energy
        pay[index, 42:43, :] = cross


def begin_kernel(
    order, source, bgt, bgc, came, local,
    residual, yn, ys, yw, ye, pay, matrix, stack, halves, product, sems,
):
    copies = []
    for index in range(NS // TALL):
        rows = pl.ds(TALL * index, TALL)
        copies.append(pltpu.make_async_copy(source.at[rows], matrix.at[rows], sems.at[index]))
        copies[-1].start()
    stacked, _ = take_values(came, stack)
    for block in range(NB):
        rows = slice(BLK * block, BLK * (block + 1))
        residual[rows, :] = local[rows, :] - jnp.dot(bgc[rows, :], stacked, preferred_element_type=f32)
    finish(order, matrix, bgt, residual, None, (yn, ys, yw, ye), pay, halves, product, copies)


def local_image(face, masks, y, near):
    if face == 0:
        return masks[0] * (y - near)
    if face == 1:
        return y - masks[1] * near
    if face == 2:
        return masks[2] * (y - near)
    return y - masks[3] * near


def scalars(first, sums, past):
    norm, energy, cross = sums
    if first:
        return norm, energy, None, norm / energy
    ratio = norm / past[0:1, :]
    curvature = energy + 2.0 * ratio * cross + ratio * ratio * past[1:2, :]
    return norm, curvature, ratio, norm / curvature


def step_kernel(first, *refs):
    order, masks, matrix, bgt, bgc, came, residual = refs[:7]
    near, faces = refs[7:11], refs[11:15]
    refs = refs[15:]
    if first:
        past = along = moved = done = image = None
    else:
        past, along, moved, image, done = refs[:5]
        refs = refs[5:]
    new_residual, new_along, new_moved, new_image, new_done, new_past = refs[:6]
    new_faces, pay, (stack, halves, product) = refs[6:10], refs[10], refs[11:]

    stacked, sums = take_values(came, stack)
    norm, curvature, ratio, step = scalars(first, sums, past)
    new_past[...] = jnp.zeros_like(new_past)
    new_past[0:1, :] = norm
    new_past[1:2, :] = curvature
    for face in range(4):
        for block in range(M // BLK):
            inside = slice(BLK * block, BLK * (block + 1))
            rows = slice(M * face + BLK * block, M * face + BLK * (block + 1))
            y = faces[face][inside, :]
            q = local_image(face, masks, y, near[face][inside, :])
            q = q - jnp.dot(bgc[rows, :], stacked, preferred_element_type=f32)
            r = residual[rows, :]
            if not first:
                q = q + ratio * moved[rows, :]
                y = y + ratio * image[rows, :]
            new_moved[rows, :] = q
            new_image[rows, :] = y
            new_residual[rows, :] = r - step * q
            if face % 2:
                own = slice(M * (face // 2) + BLK * block, M * (face // 2) + BLK * (block + 1))
                if first:
                    new_along[own, :] = r
                    new_done[own, :] = step * r
                else:
                    d = r + ratio * along[own, :]
                    new_along[own, :] = d
                    new_done[own, :] = done[own, :] + step * d
    finish(order, matrix, bgt, new_residual, new_image, new_faces, pay, halves, product)


def end_kernel(
    masks, bgc, came, residual, ns, ne, ys, ye, past, along, moved, done,
    out_done, out_residual, stack,
):
    stacked, sums = take_values(came, stack)
    _, _, ratio, step = scalars(False, sums, past)
    for face, near, mine in ((1, ns, ys), (3, ne, ye)):
        for block in range(M // BLK):
            inside = slice(BLK * block, BLK * (block + 1))
            rows = slice(M * face + BLK * block, M * face + BLK * (block + 1))
            own = slice(M * (face // 2) + BLK * block, M * (face // 2) + BLK * (block + 1))
            q = local_image(face, masks, mine[inside, :], near[inside, :])
            q = q - jnp.dot(bgc[rows, :], stacked, preferred_element_type=f32)
            q = q + ratio * moved[rows, :]
            r = residual[rows, :]
            d = r + ratio * along[own, :]
            out_residual[face // 2, :, inside] = (r - step * q).T
            out_done[face // 2, :, inside] = (done[own, :] + step * d).T


def shape(*dims, kind=f32):
    return jax.ShapeDtypeStruct(dims, kind)


WORK = [
    pltpu.VMEM((256, K), f32),
    pltpu.VMEM((NS, 2 * K), bf16),
    pltpu.VMEM((NS, K), f32),
]
FACES = [shape(M, K)] * 4


def call(kernel, specs, outs, scratch, flops):
    return pl.pallas_call(
        kernel,
        in_specs=specs,
        out_specs=[VM] * len(outs),
        out_shape=outs,
        scratch_shapes=scratch,
        compiler_params=LIMIT,
        cost_estimate=pl.CostEstimate(flops=flops, bytes_accessed=1 << 20, transcendentals=0),
    )


def coarse_table(coarse_inverse, core):
    mine = jnp.transpose(coarse_inverse[:, 0, :, :, :, 0], (1, 0, 3, 2))
    mine = jnp.pad(mine, ((0, 0), (0, SLOT - MODES), (0, 0), (0, SLOT - MODES))).reshape(COLS, SLOT, SLOT * ROWS)
    mine = jnp.concatenate([mine, mine], axis=2)
    lines = jnp.stack([mine, cyclic(mine, "row", 1), cyclic(mine, "row", -1)])
    west = cyclic(lines, "col", 1)
    east = cyclic(lines, "col", -1)
    far = swapped(jnp.where(core[0] == 0, west, east), lambda c: c ^ 1)
    (parts,) = call(
        table_kernel,
        [SM] + [VM] * 4,
        [shape(3, CHIPS * SLOTS * SLOT, 2 * K, kind=bf16)],
        [pltpu.VMEM((CHIPS * SLOTS * SLOT, 2 * K), f32)],
        10**7,
    )(core, west, lines, east, far)
    return parts


def coarse_phase(pay, parts, core):
    own = lax.all_to_all(pay, "row", 0, 0, tiled=True)
    other = swapped(own, lambda c: c ^ 1)
    (terms,) = call(
        coarse_kernel,
        [SM] + [VM] * 3,
        [shape(CHIPS, SLOTS * SLOT, K)],
        [pltpu.VMEM((2 * K, K), f32)],
        10**8,
    )(core, parts, own, other)
    groups = [[2 * chip + which for chip in range(CHIPS)] for which in range(2)]
    return lax.all_to_all(terms, "col", 0, 0, axis_index_groups=groups, tiled=True)


def per_device(schur_blocks, rigid_modes, floating, block_order, coarse_inverse, right_side):
    order = block_order[0, 0]
    row, col = lax.axis_index("row"), lax.axis_index("col")
    core = (col % 2).astype(jnp.int32).reshape(1)
    masks = jnp.stack([row > 0, row < ROWS - 1, col > 0, col < COLS - 1]).astype(f32)
    side = right_side[0, 0]

    from_n = cyclic(side[0], "row", 1)
    from_w = cyclic(side[1], "col", 1)
    used = rigid_modes[0, 0] * floating[0, 0].astype(f32)
    near_n = shifted(used[:, M : 2 * M], "row", 1)
    near_s = shifted(used[:, :M], "row", -1)
    near_w = shifted(used[:, 3 * M :], "col", 1)
    near_e = shifted(used[:, 2 * M : 3 * M], "col", -1)
    local, pay = call(
        start_kernel,
        [SM] + [VM] * 4,
        [shape(NS, K), shape(ROWS, PAY, K)],
        [pltpu.VMEM((16, NS), f32), pltpu.VMEM((NS, 2 * K), bf16)],
        10**8,
    )(masks, used, side, from_n, from_w)
    parts = coarse_table(coarse_inverse, core)
    (bgt,) = call(
        modes_kernel, [SM] + [VM] * 5, [shape(3 * PAY, NS, kind=bf16)], [pltpu.VMEM((PAY, NS), f32)], 10**8
    )(masks, used, near_n, near_s, near_w, near_e)
    (bgc,) = call(
        spread_kernel, [VM], [shape(NS, 2 * K, kind=bf16)], [pltpu.VMEM((256, NS), f32)], 10**8
    )(bgt)
    came = coarse_phase(pay, parts, core)

    residual, *faces, pay, matrix = call(
        begin_kernel,
        [SM, pl.BlockSpec(memory_space=pl.ANY)] + [VM] * 4,
        [shape(NS, K)] + FACES + [shape(ROWS, PAY, K), shape(NS, NS, kind=bf16)],
        WORK + [pltpu.SemaphoreType.DMA((NS // TALL,))],
        2 * 10**9,
    )(order, schur_blocks[0, 0], bgt, bgc, came, local)

    state = ()
    for iteration in range(ITERS):
        near = (
            cyclic(faces[1], "row", 1),
            cyclic(faces[0], "row", -1),
            cyclic(faces[3], "col", 1),
            cyclic(faces[2], "col", -1),
        )
        came = coarse_phase(pay, parts, core)
        if iteration + 1 == ITERS:
            break
        first = iteration == 0
        given = (order, masks, matrix, bgt, bgc, came, residual, *near, *faces, *state)
        residual, along, moved, image, done, past, *faces, pay = call(
            functools.partial(step_kernel, first),
            [SM, SM] + [VM] * (len(given) - 2),
            [shape(NS, K), shape(2 * M, K), shape(NS, K), shape(NS, K), shape(2 * M, K), shape(SLOT, K)]
            + FACES
            + [shape(ROWS, PAY, K)],
            WORK,
            2 * 10**9,
        )(*given)
        state = (past, along, moved, image, done)

    past, along, moved, image, done = state
    done, residual = call(
        end_kernel,
        [SM] + [VM] * 11,
        [shape(2, K, M)] * 2,
        [pltpu.VMEM((256, K), f32)],
        10**8,
    )(masks, bgc, came, residual, near[1], near[3], faces[1], faces[3], past, along, moved, done)
    return (done[None, None], residual[None, None])


def solution(mesh):
    placed = (
        P("row", "col", None, None),
        P("row", "col", None, None),
        P("row", "col"),
        P("row", "col", None),
        P(None, "row", None, None, None, "col"),
        P("row", "col", None, None, None),
    )
    return jax.shard_map(
        per_device,
        mesh=mesh,
        in_specs=placed,
        out_specs=(P("row", "col", None, None, None), P("row", "col", None, None, None)),
        check_vma=False,
    )
```

profile of v0, /device:TPU:1, one launch (start us, length us, event | category | flops | bytes accessed | tf_op | source)
XLA Modules:
  0.0 245.1 jit_solution(10310710709930462727)
XLA Ops:
  0.6 1.0 copy.14
  1.9 2.5 %collective-permute-start.4 = (f32[32,8,128]{2,1,0:T(8,128)S(1)}, f32[32,8,128]{2,1,0:T(8,128)S(1)}, u32[]{:S(2)}, u32[]{:S(2)}) collective-permute-start(f32[32,8,128]{2,1,0:T(8,128)S(1)} %get-tuple-element.69), channel_id=1, source_target_pairs={{0,32},{32,64},{64,96},{96,128},{128,160},{160,192},{192,224},{224... | collective-permute-start | bytes 393224 | tf_op jit(solution)/shard_map/ppermute | solution.py:35
  4.4 4.0 %collective-permute-start.5 = (f32[32,8,128]{2,1,0:T(8,128)S(1)}, f32[32,8,128]{2,1,0:T(8,128)S(1)}, u32[]{:S(2)}, u32[]{:S(2)}) collective-permute-start(f32[32,8,128]{2,1,0:T(8,128)S(1)} %get-tuple-element.69), channel_id=1, source_target_pairs={{0,224},{32,0},{64,32},{96,64},{128,96},{160,128},{192,160},{224,1... | collective-permute-start | bytes 393224 | tf_op jit(solution)/shard_map/ppermute | solution.py:35
  8.4 1.1 slice_bitcast_fusion
  9.5 2.2 collective-permute-start.10
  12.9 1.3 collective-permute-start.6
  15.2 5.2 %collective-permute-done.9.from_n = f32[128,512]{1,0:T(8,128)S(1)} collective-permute-done((f32[128,512]{1,0:T(8,128)S(1)}, f32[128,512]{1,0:T(8,128)S(1)}, u32[]{:S(2)}, u32[]{:S(2)}) %collective-permute-start.9) | collective-permute-done | bytes 262176 | tf_op jit(solution)/shard_map/ppermute | solution.py:35
  20.3 1.0 copy-done.1
  21.4 1.9 shard_map.80
  23.2 1.0 copy-done.2
  24.2 5.5 %all-to-all-start = ((f32[8,48,128]{2,1,0:T(8,128)}), f32[8,48,128]{2,1,0:T(8,128)S(1)}, u32[]{:S(2)}, u32[]{:S(2)}) async-start(f32[8,48,128]{2,1,0:T(8,128)} %get-tuple-element.34), calls=%async_computation | async-start | bytes 393216 | tf_op jit(solution)/shard_map/all_to_all | solution.py:373
  30.2 9.6 %all-to-all-done.own = f32[8,48,128]{2,1,0:T(8,128)S(1)} async-done(((f32[8,48,128]{2,1,0:T(8,128)}), f32[8,48,128]{2,1,0:T(8,128)S(1)}, u32[]{:S(2)}, u32[]{:S(2)}) %all-to-all-start) | async-done | bytes 196640 | tf_op jit(solution)/shard_map/all_to_all | solution.py:373
  39.9 1.3 collective-permute-start.11
  42.2 1.2 shard_map.81
  43.5 6.7 %all-to-all-start.1 = ((f32[16,40,128]{2,1,0:T(8,128)}), f32[16,40,128]{2,1,0:T(8,128)S(1)}, u32[]{:S(2)}, u32[]{:S(2)}) async-start(f32[16,40,128]{2,1,0:T(8,128)} %shard_map.81), calls=%async_computation.1 | async-start | bytes 655360 | tf_op jit(solution)/shard_map/all_to_all | solution.py:383
  50.2 2.6 %collective-permute-start.3 = (f32[6,512]{1,0:T(8,128)S(1)}, f32[6,512]{1,0:T(8,128)S(1)}, u32[]{:S(2)}, u32[]{:S(2)}) collective-permute-start(f32[6,512]{1,0:T(8,128)S(1)} %get-tuple-element.70), channel_id=1, source_target_pairs={{1,0},{2,1},{3,2},{4,3},{5,4},{6,5},{7,6},{8,7},{9,8},{10,9},{11,1... | collective-permute-start | bytes 36872 | tf_op jit(solution)/shard_map/ppermute | solution.py:41
  52.8 3.4 %collective-permute-start.2 = (f32[6,512]{1,0:T(8,128)S(1)}, f32[6,512]{1,0:T(8,128)S(1)}, u32[]{:S(2)}, u32[]{:S(2)}) collective-permute-start(f32[6,512]{1,0:T(8,128)S(1)} %get-tuple-element.71), channel_id=1, source_target_pairs={{0,1},{1,2},{2,3},{3,4},{4,5},{5,6},{6,7},{7,8},{8,9},{9,10},{10,1... | collective-permute-start | bytes 36872 | tf_op jit(solution)/shard_map/ppermute | solution.py:41
  56.2 1.3 collective-permute-start.1
  57.5 4.0 %collective-permute-start = (f32[6,512]{1,0:T(8,128)S(1)}, f32[6,512]{1,0:T(8,128)S(1)}, u32[]{:S(2)}, u32[]{:S(2)}) collective-permute-start(f32[6,512]{1,0:T(8,128)S(1)} %get-tuple-element.73), channel_id=1, source_target_pairs={{0,32},{32,64},{64,96},{96,128},{128,160},{160,192},{192,224},{1,3... | collective-permute-start | bytes 36872 | tf_op jit(solution)/shard_map/ppermute | solution.py:41
  63.4 1.2 copy-done.3
  64.6 8.1 %shard_map.82 = (f32[2048,128]{1,0:T(8,128)S(1)}, f32[512,128]{1,0:T(8,128)S(1)}, f32[512,128]{1,0:T(8,128)S(1)}, f32[512,128]{1,0:T(8,128)S(1)}, f32[512,128]{1...) custom-call(s32[16]{0:T(128)S(1)} %bitcast.27, bf16[2048,2048]{1,0:T(8,128)(2,1)} %bitcast.30, ...), custom_call_target="tpu_custom_call" | custom-call | flops 2000000000 | bytes 1048576 | tf_op jit(solution)/shard_map/pallas_call | solution.py:416
  72.7 3.3 %copy-done = bf16[2048,2048]{1,0:T(8,128)(2,1)} copy-done((bf16[2048,2048]{1,0:T(8,128)(2,1)}, bf16[2048,2048]{1,0:T(8,128)(2,1)S(1)}, u32[]{:S(2)}) %copy-start) | copy-done | bytes 8388632
  76.1 1.0 copy-done.14
  79.2 14.6 %all_to_all.40.own = f32[8,48,128]{2,1,0:T(8,128)S(1)} all-to-all(f32[8,48,128]{2,1,0:T(8,128)S(1)} %get-tuple-element.37), channel_id=1, replica_groups=mesh['row'=8,'col'=32] {'row'}, dimensions={0} | all-to-all | bytes 393216 | tf_op jit(solution)/shard_map/all_to_all | solution.py:373
  93.8 2.0 collective-permute-start.12
  95.8 1.1 collective-permute-done.12.other
  96.9 1.2 shard_map.83
  98.1 7.7 %all-to-all-start.3 = ((f32[16,40,128]{2,1,0:T(8,128)}), f32[16,40,128]{2,1,0:T(8,128)S(1)}, u32[]{:S(2)}, u32[]{:S(2)}) async-start(f32[16,40,128]{2,1,0:T(8,128)} %shard_map.83), calls=%async_computation.3 | async-start | bytes 655360 | tf_op jit(solution)/shard_map/all_to_all | solution.py:383
  105.9 2.6 %collective-permute-start.14 = (f32[512,128]{1,0:T(8,128)}, f32[512,128]{1,0:T(8,128)S(1)}, u32[]{:S(2)}, u32[]{:S(2)}) collective-permute-start(f32[512,128]{1,0:T(8,128)} %copy-done.38), channel_id=1, source_target_pairs={{0,224},{32,0},{64,32},{96,64},{128,96},{160,128},{192,160},{224,1... | collective-permute-start | bytes 786440 | tf_op jit(solution)/shard_map/ppermute | solution.py:35
  108.6 2.7 %collective-permute-start.15 = (f32[512,128]{1,0:T(8,128)}, f32[512,128]{1,0:T(8,128)S(1)}, u32[]{:S(2)}, u32[]{:S(2)}) collective-permute-start(f32[512,128]{1,0:T(8,128)} %copy-done.44), channel_id=1, source_target_pairs={{0,1},{1,2},{2,3},{3,4},{4,5},{5,6},{6,7},{7,8},{8,9},{9,10},{10,1... | collective-permute-start | bytes 786440 | tf_op jit(solution)/shard_map/ppermute | solution.py:35
  111.2 3.3 %collective-permute-done.13.refs_7_ = f32[512,128]{1,0:T(8,128)S(1)} collective-permute-done((f32[512,128]{1,0:T(8,128)}, f32[512,128]{1,0:T(8,128)S(1)}, u32[]{:S(2)}, u32[]{:S(2)}) %collective-permute-start.13) | collective-permute-done | bytes 262176 | tf_op jit(solution)/shard_map/ppermute | solution.py:35
  118.2 1.2 copy-done.15
  127.1 7.5 %shard_map.84 = (f32[2048,128]{1,0:T(8,128)S(1)}, f32[1024,128]{1,0:T(8,128)S(1)}, f32[2048,128]{1,0:T(8,128)S(1)}, f32[2048,128]{1,0:T(8,128)S(1)}, f32[1024,12...) custom-call(s32[16]{0:T(128)S(1)} %bitcast.28, ...), custom_call_target="tpu_custom_call" | custom-call | flops 2000000000 | bytes 1048576 | tf_op jit(solution)/shard_map/pallas_call | solution.py:437
  134.6 1.0 copy-done.4
  135.6 1.0 copy-done.6
  136.6 1.0 copy-done.8
  140.5 11.0 %all_to_all.41.own = f32[8,48,128]{2,1,0:T(8,128)S(1)} all-to-all(f32[8,48,128]{2,1,0:T(8,128)S(1)} %get-tuple-element.43), channel_id=1, replica_groups=mesh['row'=8,'col'=32] {'row'}, dimensions={0} | all-to-all | bytes 393216 | tf_op jit(solution)/shard_map/all_to_all | solution.py:373
  151.6 3.4 %collective-permute-start.17 = (f32[8,48,128]{2,1,0:T(8,128)S(1)}, f32[8,48,128]{2,1,0:T(8,128)S(1)}, u32[]{:S(2)}, u32[]{:S(2)}) collective-permute-start(f32[8,48,128]{2,1,0:T(8,128)S(1)} %all_to_all.41.own), channel_id=1, source_target_pairs={{0,1},{1,0},{2,3},{3,2},{4,5},{5,4},{6,7},{7,6},{8,9},{9,8},{10,11... | collective-permute-start | bytes 589832 | tf_op jit(solution)/shard_map/ppermute | solution.py:45
  154.9 1.1 collective-permute-done.17.other
  156.0 1.2 shard_map.85
  157.3 7.1 %all-to-all-start.5 = ((f32[16,40,128]{2,1,0:T(8,128)}), f32[16,40,128]{2,1,0:T(8,128)S(1)}, u32[]{:S(2)}, u32[]{:S(2)}) async-start(f32[16,40,128]{2,1,0:T(8,128)} %shard_map.85), calls=%async_computation.5 | async-start | bytes 655360 | tf_op jit(solution)/shard_map/all_to_all | solution.py:383
  164.7 2.4 collective-permute-start.19
  167.1 2.7 %collective-permute-start.20 = (f32[512,128]{1,0:T(8,128)}, f32[512,128]{1,0:T(8,128)S(1)}, u32[]{:S(2)}, u32[]{:S(2)}) collective-permute-start(f32[512,128]{1,0:T(8,128)} %copy-done.28), channel_id=1, source_target_pairs={{0,1},{1,2},{2,3},{3,4},{4,5},{5,6},{6,7},{7,8},{8,9},{9,10},{10,1... | collective-permute-start | bytes 786440 | tf_op jit(solution)/shard_map/ppermute | solution.py:35
  169.8 3.3 %collective-permute-done.18.refs_7_ = f32[512,128]{1,0:T(8,128)S(1)} collective-permute-done((f32[512,128]{1,0:T(8,128)}, f32[512,128]{1,0:T(8,128)S(1)}, u32[]{:S(2)}, u32[]{:S(2)}) %collective-permute-start.18) | collective-permute-done | bytes 262176 | tf_op jit(solution)/shard_map/ppermute | solution.py:35
  175.1 0.9 collective-permute-done.21.refs_10_
  176.8 1.2 copy-done.5
  178.0 1.2 copy-done.7
  179.3 1.2 copy-done.9
  180.5 1.0 copy-done.17
  189.1 8.5 %shard_map.86 = (f32[2048,128]{1,0:T(8,128)S(1)}, f32[1024,128]{1,0:T(8,128)S(1)}, f32[2048,128]{1,0:T(8,128)S(1)}, f32[2048,128]{1,0:T(8,128)}, f32[1024,128]{1...) custom-call(s32[16]{0:T(128)S(1)} %bitcast.29, ...), custom_call_target="tpu_custom_call" | custom-call | flops 2000000000 | bytes 1048576 | tf_op jit(solution)/shard_map/pallas_call | solution.py:437
  197.7 1.0 copy-done.10
  198.6 1.0 copy-done.12
  203.3 11.0 %all_to_all.42.own = f32[8,48,128]{2,1,0:T(8,128)S(1)} all-to-all(f32[8,48,128]{2,1,0:T(8,128)S(1)} %get-tuple-element.54), channel_id=1, replica_groups=mesh['row'=8,'col'=32] {'row'}, dimensions={0} | all-to-all | bytes 393216 | tf_op jit(solution)/shard_map/all_to_all | solution.py:373
  214.3 3.4 %collective-permute-start.22 = (f32[8,48,128]{2,1,0:T(8,128)S(1)}, f32[8,48,128]{2,1,0:T(8,128)S(1)}, u32[]{:S(2)}, u32[]{:S(2)}) collective-permute-start(f32[8,48,128]{2,1,0:T(8,128)S(1)} %all_to_all.42.own), channel_id=1, source_target_pairs={{0,1},{1,0},{2,3},{3,2},{4,5},{5,4},{6,7},{7,6},{8,9},{9,8},{10,11... | collective-permute-start | bytes 589832 | tf_op jit(solution)/shard_map/ppermute | solution.py:45
  217.7 1.1 collective-permute-done.22.other
  218.8 1.3 shard_map.87
  220.0 7.1 %all-to-all-start.7 = ((f32[16,40,128]{2,1,0:T(8,128)}), f32[16,40,128]{2,1,0:T(8,128)S(1)}, u32[]{:S(2)}, u32[]{:S(2)}) async-start(f32[16,40,128]{2,1,0:T(8,128)} %shard_map.87), calls=%async_computation.7 | async-start | bytes 655360 | tf_op jit(solution)/shard_map/all_to_all | solution.py:383
  228.0 6.7 %collective-permute-done.23.ns = f32[512,128]{1,0:T(8,128)S(1)} collective-permute-done((f32[512,128]{1,0:T(8,128)}, f32[512,128]{1,0:T(8,128)S(1)}, u32[]{:S(2)}, u32[]{:S(2)}) %collective-permute-start.23) | collective-permute-done | bytes 262176 | tf_op jit(solution)/shard_map/ppermute | solution.py:35
  234.6 2.0 collective-permute-done.24.ne
  236.7 1.2 copy-done.11
  237.9 1.2 copy-done.13
  239.1 1.0 copy-done.19
  240.2 1.0 copy-done.21
  243.1 2.0 shard_map.88
  (143 shorter events, 38.7 us)
Async XLA Ops:
  0.6 62.8 %copy-start.58 = (s32[1,1,16]{2,1,0:T(1,128)S(1)}, s32[1,1,16]{2,1,0:T(1,128)}, u32[]{:S(2)}) copy-start(s32[1,1,16]{2,1,0:T(1,128)} %param.9) | copy-start | bytes 196
  1.9 10.5 %collective-permute-start.4 = (f32[32,8,128]{2,1,0:T(8,128)S(1)}, f32[32,8,128]{2,1,0:T(8,128)S(1)}, u32[]{:S(2)}, u32[]{:S(2)}) collective-permute-start(f32[32,8,128]{2,1,0:T(8,128)S(1)} %get-tuple-element.69), channel_id=1, source_target_pairs={{0,32},{32,64},{64,96},{96,128},{128,160},{160,192},{192,224},{224... | collective-permute-start | bytes 393224 | tf_op jit(solution)/shard_map/ppermute | solution.py:35
  4.4 8.0 %collective-permute-start.5 = (f32[32,8,128]{2,1,0:T(8,128)S(1)}, f32[32,8,128]{2,1,0:T(8,128)S(1)}, u32[]{:S(2)}, u32[]{:S(2)}) collective-permute-start(f32[32,8,128]{2,1,0:T(8,128)S(1)} %get-tuple-element.69), channel_id=1, source_target_pairs={{0,224},{32,0},{64,32},{96,64},{128,96},{160,128},{192,160},{224,1... | collective-permute-start | bytes 393224 | tf_op jit(solution)/shard_map/ppermute | solution.py:35
  9.5 5.7 %collective-permute-start.10 = (f32[128,512]{1,0:T(8,128)S(1)}, f32[128,512]{1,0:T(8,128)S(1)}, u32[]{:S(2)}, u32[]{:S(2)}) collective-permute-start(f32[128,512]{1,0:T(8,128)S(1)} %get-tuple-element.66), channel_id=1, source_target_pairs={{0,1},{1,2},{2,3},{3,4},{4,5},{5,6},{6,7},{7,8},{8,9},{9,10},{10,1... | collective-permute-start | bytes 786440 | tf_op jit(solution)/shard_map/ppermute | solution.py:35
  11.7 8.6 %collective-permute-start.9 = (f32[128,512]{1,0:T(8,128)S(1)}, f32[128,512]{1,0:T(8,128)S(1)}, u32[]{:S(2)}, u32[]{:S(2)}) collective-permute-start(f32[128,512]{1,0:T(8,128)S(1)} %get-tuple-element.67), channel_id=1, source_target_pairs={{0,32},{32,64},{64,96},{96,128},{128,160},{160,192},{192,224},{224... | collective-permute-start | bytes 786440 | tf_op jit(solution)/shard_map/ppermute | solution.py:35
  12.4 17.3 %collective-permute-start.7 = (f32[3,32,8,128]{3,2,1,0:T(8,128)S(1)}, f32[3,32,8,128]{3,2,1,0:T(8,128)S(1)}, u32[]{:S(2)}, u32[]{:S(2)}) collective-permute-start(f32[3,32,8,128]{3,2,1,0:T(8,128)S(1)} %pad_maximum_fusion.mine), channel_id=1, source_target_pairs={{0,31},{1,0},{2,1},{3,2},{4,3},{5,4},{6,5},{7,6},{8,7},{9,8},{10,9... | collective-permute-start | bytes 1179656 | tf_op jit(solution)/shard_map/ppermute | solution.py:35
  12.9 16.8 %collective-permute-start.6 = (f32[3,32,8,128]{3,2,1,0:T(8,128)S(1)}, f32[3,32,8,128]{3,2,1,0:T(8,128)S(1)}, u32[]{:S(2)}, u32[]{:S(2)}) collective-permute-start(f32[3,32,8,128]{3,2,1,0:T(8,128)S(1)} %pad_maximum_fusion.mine), channel_id=1, source_target_pairs={{0,1},{1,2},{2,3},{3,4},{4,5},{5,6},{6,7},{7,8},{8,9},{9,10},{10,1... | collective-permute-start | bytes 1179656 | tf_op jit(solution)/shard_map/ppermute | solution.py:35
  20.3 1.0 copy-start.1
  23.2 1.0 copy-start.2
  24.2 15.6 %all-to-all-start = ((f32[8,48,128]{2,1,0:T(8,128)}), f32[8,48,128]{2,1,0:T(8,128)S(1)}, u32[]{:S(2)}, u32[]{:S(2)}) async-start(f32[8,48,128]{2,1,0:T(8,128)} %get-tuple-element.34), calls=%async_computation | async-start | bytes 393216 | tf_op jit(solution)/shard_map/all_to_all | solution.py:373
  29.8 11.4 %collective-permute-start.8 = (f32[3,32,8,128]{3,2,1,0:T(8,128)S(1)}, f32[3,32,8,128]{3,2,1,0:T(8,128)S(1)}, u32[]{:S(2)}, u32[]{:S(2)}) collective-permute-start(f32[3,32,8,128]{3,2,1,0:T(8,128)S(1)} %broadcast_select_fusion), channel_id=1, source_target_pairs={{0,1},{1,0},{2,3},{3,2},{4,5},{5,4},{6,7},{7,6},{8,9},{9,8},{10,11... | collective-permute-start | bytes 1179656 | tf_op jit(solution)/shard_map/ppermute | solution.py:45
  39.9 2.4 collective-permute-start.11
  43.5 19.9 %all-to-all-start.1 = ((f32[16,40,128]{2,1,0:T(8,128)}), f32[16,40,128]{2,1,0:T(8,128)S(1)}, u32[]{:S(2)}, u32[]{:S(2)}) async-start(f32[16,40,128]{2,1,0:T(8,128)} %shard_map.81), calls=%async_computation.1 | async-start | bytes 655360 | tf_op jit(solution)/shard_map/all_to_all | solution.py:383
  50.2 11.3 %collective-permute-start.3 = (f32[6,512]{1,0:T(8,128)S(1)}, f32[6,512]{1,0:T(8,128)S(1)}, u32[]{:S(2)}, u32[]{:S(2)}) collective-permute-start(f32[6,512]{1,0:T(8,128)S(1)} %get-tuple-element.70), channel_id=1, source_target_pairs={{1,0},{2,1},{3,2},{4,3},{5,4},{6,5},{7,6},{8,7},{9,8},{10,9},{11,1... | collective-permute-start | bytes 36872 | tf_op jit(solution)/shard_map/ppermute | solution.py:41
  52.8 8.8 %collective-permute-start.2 = (f32[6,512]{1,0:T(8,128)S(1)}, f32[6,512]{1,0:T(8,128)S(1)}, u32[]{:S(2)}, u32[]{:S(2)}) collective-permute-start(f32[6,512]{1,0:T(8,128)S(1)} %get-tuple-element.71), channel_id=1, source_target_pairs={{0,1},{1,2},{2,3},{3,4},{4,5},{5,6},{6,7},{7,8},{8,9},{9,10},{10,1... | collective-permute-start | bytes 36872 | tf_op jit(solution)/shard_map/ppermute | solution.py:41
  56.2 5.3 %collective-permute-start.1 = (f32[6,512]{1,0:T(8,128)S(1)}, f32[6,512]{1,0:T(8,128)S(1)}, u32[]{:S(2)}, u32[]{:S(2)}) collective-permute-start(f32[6,512]{1,0:T(8,128)S(1)} %get-tuple-element.72), channel_id=1, source_target_pairs={{32,0},{64,32},{96,64},{128,96},{160,128},{192,160},{224,192},{33,... | collective-permute-start | bytes 36872 | tf_op jit(solution)/shard_map/ppermute | solution.py:41
  57.5 4.8 %collective-permute-start = (f32[6,512]{1,0:T(8,128)S(1)}, f32[6,512]{1,0:T(8,128)S(1)}, u32[]{:S(2)}, u32[]{:S(2)}) collective-permute-start(f32[6,512]{1,0:T(8,128)S(1)} %get-tuple-element.73), channel_id=1, source_target_pairs={{0,32},{32,64},{64,96},{96,128},{128,160},{160,192},{192,224},{1,3... | collective-permute-start | bytes 36872 | tf_op jit(solution)/shard_map/ppermute | solution.py:41
  63.4 1.2 copy-start.3
  72.7 3.3 %copy-start = (bf16[2048,2048]{1,0:T(8,128)(2,1)}, bf16[2048,2048]{1,0:T(8,128)(2,1)S(1)}, u32[]{:S(2)}) copy-start(bf16[2048,2048]{1,0:T(8,128)(2,1)S(1)} %get-tuple-element.36.refs_2_) | copy-start | bytes 25165828
  76.1 1.0 copy-start.14
  79.2 17.7 %copy-start.38 = (f32[512,128]{1,0:T(8,128)}, f32[512,128]{1,0:T(8,128)S(1)}, u32[]{:S(2)}) copy-start(f32[512,128]{1,0:T(8,128)S(1)} %get-tuple-element.40.refs_11_) | copy-start | bytes 786436
  93.8 3.1 %collective-permute-start.12 = (f32[8,48,128]{2,1,0:T(8,128)S(1)}, f32[8,48,128]{2,1,0:T(8,128)S(1)}, u32[]{:S(2)}, u32[]{:S(2)}) collective-permute-start(f32[8,48,128]{2,1,0:T(8,128)S(1)} %all_to_all.40.own), channel_id=1, source_target_pairs={{0,1},{1,0},{2,3},{3,2},{4,5},{5,4},{6,7},{7,6},{8,9},{9,8},{10,11... | collective-permute-start | bytes 589832 | tf_op jit(solution)/shard_map/ppermute | solution.py:45
  98.1 20.1 %all-to-all-start.3 = ((f32[16,40,128]{2,1,0:T(8,128)}), f32[16,40,128]{2,1,0:T(8,128)S(1)}, u32[]{:S(2)}, u32[]{:S(2)}) async-start(f32[16,40,128]{2,1,0:T(8,128)} %shard_map.83), calls=%async_computation.3 | async-start | bytes 655360 | tf_op jit(solution)/shard_map/all_to_all | solution.py:383
  105.8 8.7 %collective-permute-start.13 = (f32[512,128]{1,0:T(8,128)}, f32[512,128]{1,0:T(8,128)S(1)}, u32[]{:S(2)}, u32[]{:S(2)}) collective-permute-start(f32[512,128]{1,0:T(8,128)} %copy-done.40), channel_id=1, source_target_pairs={{0,32},{32,64},{64,96},{96,128},{128,160},{160,192},{192,224},{224... | collective-permute-start | bytes 786440 | tf_op jit(solution)/shard_map/ppermute | solution.py:35
  105.9 9.3 %collective-permute-start.14 = (f32[512,128]{1,0:T(8,128)}, f32[512,128]{1,0:T(8,128)S(1)}, u32[]{:S(2)}, u32[]{:S(2)}) collective-permute-start(f32[512,128]{1,0:T(8,128)} %copy-done.38), channel_id=1, source_target_pairs={{0,224},{32,0},{64,32},{96,64},{128,96},{160,128},{192,160},{224,1... | collective-permute-start | bytes 786440 | tf_op jit(solution)/shard_map/ppermute | solution.py:35
  108.6 7.3 %collective-permute-start.15 = (f32[512,128]{1,0:T(8,128)}, f32[512,128]{1,0:T(8,128)S(1)}, u32[]{:S(2)}, u32[]{:S(2)}) collective-permute-start(f32[512,128]{1,0:T(8,128)} %copy-done.44), channel_id=1, source_target_pairs={{0,1},{1,2},{2,3},{3,4},{4,5},{5,6},{6,7},{7,8},{8,9},{9,10},{10,1... | collective-permute-start | bytes 786440 | tf_op jit(solution)/shard_map/ppermute | solution.py:35
  111.2 6.3 %collective-permute-start.16 = (f32[512,128]{1,0:T(8,128)}, f32[512,128]{1,0:T(8,128)S(1)}, u32[]{:S(2)}, u32[]{:S(2)}) collective-permute-start(f32[512,128]{1,0:T(8,128)} %copy-done.42), channel_id=1, source_target_pairs={{0,31},{1,0},{2,1},{3,2},{4,3},{5,4},{6,5},{7,6},{8,7},{9,8},{10,9... | collective-permute-start | bytes 786440 | tf_op jit(solution)/shard_map/ppermute | solution.py:35
  118.2 1.2 copy-start.15
  119.5 0.9 copy-start.39
  120.4 0.9 copy-start.41
  121.4 0.9 copy-start.43
  122.3 0.9 copy-start.45
  123.3 0.9 copy-start.51
  124.2 0.9 copy-start.53
  125.2 0.9 copy-start.55
  126.1 0.9 copy-start.57
  134.6 1.0 copy-start.4
  135.6 1.0 copy-start.6
  136.6 1.0 copy-start.8
  140.5 15.5 %copy-start.22 = (f32[512,128]{1,0:T(8,128)}, f32[512,128]{1,0:T(8,128)S(1)}, u32[]{:S(2)}) copy-start(f32[512,128]{1,0:T(8,128)S(1)} %get-tuple-element.46.refs_11_) | copy-start | bytes 786436
  151.6 4.4 %collective-permute-start.17 = (f32[8,48,128]{2,1,0:T(8,128)S(1)}, f32[8,48,128]{2,1,0:T(8,128)S(1)}, u32[]{:S(2)}, u32[]{:S(2)}) collective-permute-start(f32[8,48,128]{2,1,0:T(8,128)S(1)} %all_to_all.41.own), channel_id=1, source_target_pairs={{0,1},{1,0},{2,3},{3,2},{4,5},{5,4},{6,7},{7,6},{8,9},{9,8},{10,11... | collective-permute-start | bytes 589832 | tf_op jit(solution)/shard_map/ppermute | solution.py:45
  157.3 19.6 %all-to-all-start.5 = ((f32[16,40,128]{2,1,0:T(8,128)}), f32[16,40,128]{2,1,0:T(8,128)S(1)}, u32[]{:S(2)}, u32[]{:S(2)}) async-start(f32[16,40,128]{2,1,0:T(8,128)} %shard_map.85), calls=%async_computation.5 | async-start | bytes 655360 | tf_op jit(solution)/shard_map/all_to_all | solution.py:383
  164.4 8.7 %collective-permute-start.18 = (f32[512,128]{1,0:T(8,128)}, f32[512,128]{1,0:T(8,128)S(1)}, u32[]{:S(2)}, u32[]{:S(2)}) collective-permute-start(f32[512,128]{1,0:T(8,128)} %copy-done.24), channel_id=1, source_target_pairs={{0,32},{32,64},{64,96},{96,128},{128,160},{160,192},{192,224},{224... | collective-permute-start | bytes 786440 | tf_op jit(solution)/shard_map/ppermute | solution.py:35
  164.7 9.0 %collective-permute-start.19 = (f32[512,128]{1,0:T(8,128)}, f32[512,128]{1,0:T(8,128)S(1)}, u32[]{:S(2)}, u32[]{:S(2)}) collective-permute-start(f32[512,128]{1,0:T(8,128)} %copy-done.22), channel_id=1, source_target_pairs={{0,224},{32,0},{64,32},{96,64},{128,96},{160,128},{192,160},{224,1... | collective-permute-start | bytes 786440 | tf_op jit(solution)/shard_map/ppermute | solution.py:35
  167.1 7.3 %collective-permute-start.20 = (f32[512,128]{1,0:T(8,128)}, f32[512,128]{1,0:T(8,128)S(1)}, u32[]{:S(2)}, u32[]{:S(2)}) collective-permute-start(f32[512,128]{1,0:T(8,128)} %copy-done.28), channel_id=1, source_target_pairs={{0,1},{1,2},{2,3},{3,4},{4,5},{5,6},{6,7},{7,8},{8,9},{9,10},{10,1... | collective-permute-start | bytes 786440 | tf_op jit(solution)/shard_map/ppermute | solution.py:35
  169.8 6.3 %collective-permute-start.21 = (f32[512,128]{1,0:T(8,128)}, f32[512,128]{1,0:T(8,128)S(1)}, u32[]{:S(2)}, u32[]{:S(2)}) collective-permute-start(f32[512,128]{1,0:T(8,128)} %copy-done.26), channel_id=1, source_target_pairs={{0,31},{1,0},{2,1},{3,2},{4,3},{5,4},{6,5},{7,6},{8,7},{9,8},{10,9... | collective-permute-start | bytes 786440 | tf_op jit(solution)/shard_map/ppermute | solution.py:35
  176.8 1.2 copy-start.5
  178.0 1.2 copy-start.7
  179.3 1.2 copy-start.9
  180.5 1.0 copy-start.17
  181.5 0.9 copy-start.23
  182.5 0.9 copy-start.25
  183.4 0.9 copy-start.27
  197.6 1.0 copy-start.10
  198.6 1.0 copy-start.12
  203.3 15.5 %copy-start.46 = (f32[512,128]{1,0:T(8,128)}, f32[512,128]{1,0:T(8,128)S(1)}, u32[]{:S(2)}) copy-start(f32[512,128]{1,0:T(8,128)S(1)} %get-tuple-element.58.ys) | copy-start | bytes 786436
  214.3 4.4 %collective-permute-start.22 = (f32[8,48,128]{2,1,0:T(8,128)S(1)}, f32[8,48,128]{2,1,0:T(8,128)S(1)}, u32[]{:S(2)}, u32[]{:S(2)}) collective-permute-start(f32[8,48,128]{2,1,0:T(8,128)S(1)} %all_to_all.42.own), channel_id=1, source_target_pairs={{0,1},{1,0},{2,3},{3,2},{4,5},{5,4},{6,7},{7,6},{8,9},{9,8},{10,11... | collective-permute-start | bytes 589832 | tf_op jit(solution)/shard_map/ppermute | solution.py:45
  220.0 16.6 %all-to-all-start.7 = ((f32[16,40,128]{2,1,0:T(8,128)}), f32[16,40,128]{2,1,0:T(8,128)S(1)}, u32[]{:S(2)}, u32[]{:S(2)}) async-start(f32[16,40,128]{2,1,0:T(8,128)} %shard_map.87), calls=%async_computation.7 | async-start | bytes 655360 | tf_op jit(solution)/shard_map/all_to_all | solution.py:383
  227.2 7.5 %collective-permute-start.23 = (f32[512,128]{1,0:T(8,128)}, f32[512,128]{1,0:T(8,128)S(1)}, u32[]{:S(2)}, u32[]{:S(2)}) collective-permute-start(f32[512,128]{1,0:T(8,128)} %copy-done.60), channel_id=1, source_target_pairs={{0,224},{32,0},{64,32},{96,64},{128,96},{160,128},{192,160},{224,1... | collective-permute-start | bytes 786440 | tf_op jit(solution)/shard_map/ppermute | solution.py:35
  227.2 9.4 %collective-permute-start.24 = (f32[512,128]{1,0:T(8,128)}, f32[512,128]{1,0:T(8,128)S(1)}, u32[]{:S(2)}, u32[]{:S(2)}) collective-permute-start(f32[512,128]{1,0:T(8,128)} %copy-done.59), channel_id=1, source_target_pairs={{0,31},{1,0},{2,1},{3,2},{4,3},{5,4},{6,5},{7,6},{8,7},{9,8},{10,9... | collective-permute-start | bytes 786440 | tf_op jit(solution)/shard_map/ppermute | solution.py:35
  236.7 1.2 copy-start.11
  237.9 1.2 copy-start.13
  239.1 1.0 copy-start.19
  240.2 1.0 copy-start.21
  (27 other events, 21.0 us)
where the time goes:
time: 247 us; the launch traced here: 245 us
  starting transfers between devices  78.2 us (32%)
  local copies, waits for them, and re-layouts  56.5 us (23%)
  waiting for transfers between devices  36.8 us (15%)
  blocking collectives  36.7 us (15%)
  Pallas kernels  34.2 us (14%)
    unnamed x123, local copies, waits for them, and re-layouts  55.3 us
    all_to_all x3, blocking collectives, coarse_phase(): own = lax.all_to_all(pay, 'row', 0, 0, tiled=True)  36.7 us
    all_to_all x4, starting transfers between devices, coarse_phase(): lax.all_to_all(terms, 'col', 0, 0, axis_index_groups=groups, tiled=True)  28.6 us
    ppermute x16, waiting for transfers between devices, cyclic(): lax.ppermute(value, axis, [(s, (s + steps) % count) for s in range(count)])  22.3 us
    ppermute x16, starting transfers between devices, cyclic(): lax.ppermute(value, axis, [(s, (s + steps) % count) for s in range(count)])  22.3 us
    pallas_call x2, Pallas kernels, per_device(): call(functools.partial(step_kernel, first), [SM, SM] + [VM] * (len(given)...  16 us
    ppermute x4, starting transfers between devices, shifted(): lax.ppermute(value, axis, [(s, s + steps) for s in range(initial, last)])  11.3 us
    ppermute x5, starting transfers between devices, swapped(): return lax.ppermute(value, 'col', [(s, partner(s)) for s in range(COLS)])  10.5 us
  transfers between devices with their start and end apart: 30, of which 13 were waited for; matrix products, arithmetic and copies ran while one was open for 1% of the time, Pallas kernels for 1%

commit v1 on v0

--- a/solution.py
+++ b/solution.py
@@ -27,7 +27,7 @@
 bf16 = jnp.bfloat16
 VM = pl.BlockSpec(memory_space=pltpu.VMEM)
 SM = pl.BlockSpec(memory_space=pltpu.SMEM)
-LIMIT = pltpu.CompilerParams(vmem_limit_bytes=40 * 1024 * 1024)
+LIMIT = pltpu.CompilerParams(vmem_limit_bytes=12 * 1024 * 1024)
 
 
 def cyclic(value, axis, steps):

time: 247 us -> 251 us (1.016)
  local copies, waits for them, and re-layouts: 56.5 us -> 66.8 us
  Pallas kernels: 34.2 us -> 27.6 us
    unnamed x123 -> x129, local copies, waits for them, and re-layouts: 55.3 us -> 65.5 us
    pallas_call x2, Pallas kernels: 16 us -> 10.3 us  [per_device(): call(functools.partial(step_kernel, first), [SM, SM] + [VM] * (len(given)...]
where the time goes in v1:
time: 251 us; the launch traced here: 249 us
  starting transfers between devices  78.2 us (31%)
  local copies, waits for them, and re-layouts  66.8 us (27%)
  waiting for transfers between devices  36.7 us (15%)
  blocking collectives  36.7 us (15%)
  Pallas kernels  27.6 us (11%)
    unnamed x129, local copies, waits for them, and re-layouts  65.5 us
    all_to_all x3, blocking collectives, coarse_phase(): own = lax.all_to_all(pay, 'row', 0, 0, tiled=True)  36.7 us
    all_to_all x4, starting transfers between devices, coarse_phase(): lax.all_to_all(terms, 'col', 0, 0, axis_index_groups=groups, tiled=True)  28.6 us
    ppermute x16, starting transfers between devices, cyclic(): lax.ppermute(value, axis, [(s, (s + steps) % count) for s in range(count)])  22.3 us
    ppermute x16, waiting for transfers between devices, cyclic(): lax.ppermute(value, axis, [(s, (s + steps) % count) for s in range(count)])  22.2 us
    ppermute x4, starting transfers between devices, shifted(): lax.ppermute(value, axis, [(s, s + steps) for s in range(initial, last)])  11.3 us
    ppermute x5, starting transfers between devices, swapped(): return lax.ppermute(value, 'col', [(s, partner(s)) for s in range(COLS)])  10.6 us
    pallas_call x2, Pallas kernels, per_device(): call(functools.partial(step_kernel, first), [SM, SM] + [VM] * (len(given)...  10.3 us
  transfers between devices with their start and end apart: 30, of which 13 were waited for; matrix products, arithmetic and copies ran while one was open for 1% of the time, Pallas kernels for 1%

profile of v1, /device:TPU:1, one launch (start us, length us, event | category | flops | bytes accessed | tf_op | source)
XLA Modules:
  0.0 248.7 jit_solution(7382748445852355498)
XLA Ops:
  1.9 2.5 %collective-permute-start.4 = (f32[32,8,128]{2,1,0:T(8,128)S(1)}, f32[32,8,128]{2,1,0:T(8,128)S(1)}, u32[]{:S(2)}, u32[]{:S(2)}) collective-permute-start(f32[32,8,128]{2,1,0:T(8,128)S(1)} %get-tuple-element.69), channel_id=1, source_target_pairs={{0,32},{32,64},{64,96},{96,128},{128,160},{160,192},{192,224},{224... | collective-permute-start | bytes 393224 | tf_op jit(solution)/shard_map/ppermute | solution.py:35
  4.4 4.0 %collective-permute-start.5 = (f32[32,8,128]{2,1,0:T(8,128)S(1)}, f32[32,8,128]{2,1,0:T(8,128)S(1)}, u32[]{:S(2)}, u32[]{:S(2)}) collective-permute-start(f32[32,8,128]{2,1,0:T(8,128)S(1)} %get-tuple-element.69), channel_id=1, source_target_pairs={{0,224},{32,0},{64,32},{96,64},{128,96},{160,128},{192,160},{224,1... | collective-permute-start | bytes 393224 | tf_op jit(solution)/shard_map/ppermute | solution.py:35
  8.4 1.1 slice_bitcast_fusion
  9.5 2.2 collective-permute-start.10
  12.9 1.3 collective-permute-start.6
  15.2 5.2 %collective-permute-done.9.from_n = f32[128,512]{1,0:T(8,128)S(1)} collective-permute-done((f32[128,512]{1,0:T(8,128)S(1)}, f32[128,512]{1,0:T(8,128)S(1)}, u32[]{:S(2)}, u32[]{:S(2)}) %collective-permute-start.9) | collective-permute-done | bytes 262176 | tf_op jit(solution)/shard_map/ppermute | solution.py:35
  20.3 1.0 copy-done.4
  21.4 1.9 shard_map.80
  23.2 1.0 copy-done.5
  24.2 5.5 %all-to-all-start = ((f32[8,48,128]{2,1,0:T(8,128)}), f32[8,48,128]{2,1,0:T(8,128)S(1)}, u32[]{:S(2)}, u32[]{:S(2)}) async-start(f32[8,48,128]{2,1,0:T(8,128)} %get-tuple-element.34), calls=%async_computation | async-start | bytes 393216 | tf_op jit(solution)/shard_map/all_to_all | solution.py:373
  30.2 9.6 %all-to-all-done.own = f32[8,48,128]{2,1,0:T(8,128)S(1)} async-done(((f32[8,48,128]{2,1,0:T(8,128)}), f32[8,48,128]{2,1,0:T(8,128)S(1)}, u32[]{:S(2)}, u32[]{:S(2)}) %all-to-all-start) | async-done | bytes 196640 | tf_op jit(solution)/shard_map/all_to_all | solution.py:373
  39.9 1.3 collective-permute-start.11
  42.2 1.2 shard_map.81
  43.5 6.7 %all-to-all-start.1 = ((f32[16,40,128]{2,1,0:T(8,128)}), f32[16,40,128]{2,1,0:T(8,128)S(1)}, u32[]{:S(2)}, u32[]{:S(2)}) async-start(f32[16,40,128]{2,1,0:T(8,128)} %shard_map.81), calls=%async_computation.1 | async-start | bytes 655360 | tf_op jit(solution)/shard_map/all_to_all | solution.py:383
  50.2 2.6 %collective-permute-start.3 = (f32[6,512]{1,0:T(8,128)S(1)}, f32[6,512]{1,0:T(8,128)S(1)}, u32[]{:S(2)}, u32[]{:S(2)}) collective-permute-start(f32[6,512]{1,0:T(8,128)S(1)} %get-tuple-element.70), channel_id=1, source_target_pairs={{1,0},{2,1},{3,2},{4,3},{5,4},{6,5},{7,6},{8,7},{9,8},{10,9},{11,1... | collective-permute-start | bytes 36872 | tf_op jit(solution)/shard_map/ppermute | solution.py:41
  52.8 3.4 %collective-permute-start.2 = (f32[6,512]{1,0:T(8,128)S(1)}, f32[6,512]{1,0:T(8,128)S(1)}, u32[]{:S(2)}, u32[]{:S(2)}) collective-permute-start(f32[6,512]{1,0:T(8,128)S(1)} %get-tuple-element.71), channel_id=1, source_target_pairs={{0,1},{1,2},{2,3},{3,4},{4,5},{5,6},{6,7},{7,8},{8,9},{9,10},{10,1... | collective-permute-start | bytes 36872 | tf_op jit(solution)/shard_map/ppermute | solution.py:41
  56.2 1.3 collective-permute-start.1
  57.5 4.0 %collective-permute-start = (f32[6,512]{1,0:T(8,128)S(1)}, f32[6,512]{1,0:T(8,128)S(1)}, u32[]{:S(2)}, u32[]{:S(2)}) collective-permute-start(f32[6,512]{1,0:T(8,128)S(1)} %get-tuple-element.73), channel_id=1, source_target_pairs={{0,32},{32,64},{64,96},{96,128},{128,160},{160,192},{192,224},{1,3... | collective-permute-start | bytes 36872 | tf_op jit(solution)/shard_map/ppermute | solution.py:41
  63.4 3.4 %copy-done.3 = bf16[1,1,2048,2048]{3,2,1,0:T(8,128)(2,1)S(1)} copy-done((bf16[1,1,2048,2048]{3,2,1,0:T(8,128)(2,1)S(1)}, bf16[1,1,2048,2048]{3,2,1,0:T(8,128)(2,1)}, u32[]{:S(2)}) %copy-start.3) | copy-done | bytes 8388632
  66.8 1.2 copy-done.6
  68.0 7.2 %shard_map.82 = (f32[2048,128]{1,0:T(8,128)S(1)}, f32[512,128]{1,0:T(8,128)S(1)}, f32[512,128]{1,0:T(8,128)S(1)}, f32[512,128]{1,0:T(8,128)S(1)}, f32[512,128]{1...) custom-call(s32[16]{0:T(128)S(1)} %bitcast.28, bf16[2048,2048]{1,0:T(8,128)(2,1)S(1)} %bitcast.26, ...), custom_call_target="tpu_custom_call" | custom-call | flops 2000000000 | bytes 1048576 | tf_op jit(solution)/shard_map/pallas_call | solution.py:416
  75.2 3.3 %copy-done = bf16[2048,2048]{1,0:T(8,128)(2,1)} copy-done((bf16[2048,2048]{1,0:T(8,128)(2,1)}, bf16[2048,2048]{1,0:T(8,128)(2,1)S(1)}, u32[]{:S(2)}) %copy-start) | copy-done | bytes 8388632
  78.5 1.0 copy-done.17
  81.6 14.6 %all_to_all.40.own = f32[8,48,128]{2,1,0:T(8,128)S(1)} all-to-all(f32[8,48,128]{2,1,0:T(8,128)S(1)} %get-tuple-element.37), channel_id=1, replica_groups=mesh['row'=8,'col'=32] {'row'}, dimensions={0} | all-to-all | bytes 393216 | tf_op jit(solution)/shard_map/all_to_all | solution.py:373
  96.3 2.0 collective-permute-start.12
  98.3 1.1 collective-permute-done.12.other
  99.4 1.2 shard_map.83
  100.6 7.7 %all-to-all-start.3 = ((f32[16,40,128]{2,1,0:T(8,128)}), f32[16,40,128]{2,1,0:T(8,128)S(1)}, u32[]{:S(2)}, u32[]{:S(2)}) async-start(f32[16,40,128]{2,1,0:T(8,128)} %shard_map.83), calls=%async_computation.3 | async-start | bytes 655360 | tf_op jit(solution)/shard_map/all_to_all | solution.py:383
  108.5 2.6 %collective-permute-start.14 = (f32[512,128]{1,0:T(8,128)}, f32[512,128]{1,0:T(8,128)S(1)}, u32[]{:S(2)}, u32[]{:S(2)}) collective-permute-start(f32[512,128]{1,0:T(8,128)} %copy-done.41), channel_id=1, source_target_pairs={{0,224},{32,0},{64,32},{96,64},{128,96},{160,128},{192,160},{224,1... | collective-permute-start | bytes 786440 | tf_op jit(solution)/shard_map/ppermute | solution.py:35
  111.1 2.7 %collective-permute-start.15 = (f32[512,128]{1,0:T(8,128)}, f32[512,128]{1,0:T(8,128)S(1)}, u32[]{:S(2)}, u32[]{:S(2)}) collective-permute-start(f32[512,128]{1,0:T(8,128)} %copy-done.47), channel_id=1, source_target_pairs={{0,1},{1,2},{2,3},{3,4},{4,5},{5,6},{6,7},{7,8},{8,9},{9,10},{10,1... | collective-permute-start | bytes 786440 | tf_op jit(solution)/shard_map/ppermute | solution.py:35
  113.8 3.3 %collective-permute-done.13.refs_7_ = f32[512,128]{1,0:T(8,128)S(1)} collective-permute-done((f32[512,128]{1,0:T(8,128)}, f32[512,128]{1,0:T(8,128)S(1)}, u32[]{:S(2)}, u32[]{:S(2)}) %collective-permute-start.13) | collective-permute-done | bytes 262176 | tf_op jit(solution)/shard_map/ppermute | solution.py:35
  120.8 3.4 %copy-done.1 = bf16[2048,2048]{1,0:T(8,128)(2,1)S(1)} copy-done((bf16[2048,2048]{1,0:T(8,128)(2,1)S(1)}, bf16[2048,2048]{1,0:T(8,128)(2,1)}, u32[]{:S(2)}) %copy-start.1) | copy-done | bytes 8388632
  124.2 1.2 copy-done.18
  133.0 4.7 %shard_map.84 = (f32[2048,128]{1,0:T(8,128)S(1)}, f32[1024,128]{1,0:T(8,128)S(1)}, f32[2048,128]{1,0:T(8,128)S(1)}, f32[2048,128]{1,0:T(8,128)S(1)}, f32[1024,12...) custom-call(s32[16]{0:T(128)S(1)} %bitcast.29, ...), custom_call_target="tpu_custom_call" | custom-call | flops 2000000000 | bytes 1048576 | tf_op jit(solution)/shard_map/pallas_call | solution.py:437
  137.7 1.0 copy-done.7
  139.6 1.0 copy-done.11
  143.5 11.0 %all_to_all.41.own = f32[8,48,128]{2,1,0:T(8,128)S(1)} all-to-all(f32[8,48,128]{2,1,0:T(8,128)S(1)} %get-tuple-element.43), channel_id=1, replica_groups=mesh['row'=8,'col'=32] {'row'}, dimensions={0} | all-to-all | bytes 393216 | tf_op jit(solution)/shard_map/all_to_all | solution.py:373
  154.6 3.4 %collective-permute-start.17 = (f32[8,48,128]{2,1,0:T(8,128)S(1)}, f32[8,48,128]{2,1,0:T(8,128)S(1)}, u32[]{:S(2)}, u32[]{:S(2)}) collective-permute-start(f32[8,48,128]{2,1,0:T(8,128)S(1)} %all_to_all.41.own), channel_id=1, source_target_pairs={{0,1},{1,0},{2,3},{3,2},{4,5},{5,4},{6,7},{7,6},{8,9},{9,8},{10,11... | collective-permute-start | bytes 589832 | tf_op jit(solution)/shard_map/ppermute | solution.py:45
  158.0 1.1 collective-permute-done.17.other
  159.0 1.2 shard_map.85
  160.3 7.1 %all-to-all-start.5 = ((f32[16,40,128]{2,1,0:T(8,128)}), f32[16,40,128]{2,1,0:T(8,128)S(1)}, u32[]{:S(2)}, u32[]{:S(2)}) async-start(f32[16,40,128]{2,1,0:T(8,128)} %shard_map.85), calls=%async_computation.5 | async-start | bytes 655360 | tf_op jit(solution)/shard_map/all_to_all | solution.py:383
  167.8 2.4 collective-permute-start.19
  170.1 2.7 %collective-permute-start.20 = (f32[512,128]{1,0:T(8,128)}, f32[512,128]{1,0:T(8,128)S(1)}, u32[]{:S(2)}, u32[]{:S(2)}) collective-permute-start(f32[512,128]{1,0:T(8,128)} %copy-done.31), channel_id=1, source_target_pairs={{0,1},{1,2},{2,3},{3,4},{4,5},{5,6},{6,7},{7,8},{8,9},{9,10},{10,1... | collective-permute-start | bytes 786440 | tf_op jit(solution)/shard_map/ppermute | solution.py:35
  172.8 3.3 %collective-permute-done.18.refs_7_ = f32[512,128]{1,0:T(8,128)S(1)} collective-permute-done((f32[512,128]{1,0:T(8,128)}, f32[512,128]{1,0:T(8,128)S(1)}, u32[]{:S(2)}, u32[]{:S(2)}) %collective-permute-start.18) | collective-permute-done | bytes 262176 | tf_op jit(solution)/shard_map/ppermute | solution.py:35
  179.8 3.4 %copy-done.2 = bf16[2048,2048]{1,0:T(8,128)(2,1)S(1)} copy-done((bf16[2048,2048]{1,0:T(8,128)(2,1)S(1)}, bf16[2048,2048]{1,0:T(8,128)(2,1)}, u32[]{:S(2)}) %copy-start.2) | copy-done | bytes 8388632
  183.2 1.2 copy-done.8
  184.4 1.2 copy-done.10
  185.7 1.2 copy-done.12
  186.9 1.0 copy-done.20
  195.5 5.6 %shard_map.86 = (f32[2048,128]{1,0:T(8,128)S(1)}, f32[1024,128]{1,0:T(8,128)S(1)}, f32[2048,128]{1,0:T(8,128)S(1)}, f32[2048,128]{1,0:T(8,128)}, f32[1024,128]{1...) custom-call(s32[16]{0:T(128)S(1)} %bitcast.30, ...), custom_call_target="tpu_custom_call" | custom-call | flops 2000000000 | bytes 1048576 | tf_op jit(solution)/shard_map/pallas_call | solution.py:437
  201.2 1.0 copy-done.13
  202.2 1.0 copy-done.15
  206.9 11.0 %all_to_all.42.own = f32[8,48,128]{2,1,0:T(8,128)S(1)} all-to-all(f32[8,48,128]{2,1,0:T(8,128)S(1)} %get-tuple-element.54), channel_id=1, replica_groups=mesh['row'=8,'col'=32] {'row'}, dimensions={0} | all-to-all | bytes 393216 | tf_op jit(solution)/shard_map/all_to_all | solution.py:373
  217.9 3.4 %collective-permute-start.22 = (f32[8,48,128]{2,1,0:T(8,128)S(1)}, f32[8,48,128]{2,1,0:T(8,128)S(1)}, u32[]{:S(2)}, u32[]{:S(2)}) collective-permute-start(f32[8,48,128]{2,1,0:T(8,128)S(1)} %all_to_all.42.own), channel_id=1, source_target_pairs={{0,1},{1,0},{2,3},{3,2},{4,5},{5,4},{6,7},{7,6},{8,9},{9,8},{10,11... | collective-permute-start | bytes 589832 | tf_op jit(solution)/shard_map/ppermute | solution.py:45
  221.3 1.1 collective-permute-done.22.other
  222.4 1.3 shard_map.87
  223.7 7.1 %all-to-all-start.7 = ((f32[16,40,128]{2,1,0:T(8,128)}), f32[16,40,128]{2,1,0:T(8,128)S(1)}, u32[]{:S(2)}, u32[]{:S(2)}) async-start(f32[16,40,128]{2,1,0:T(8,128)} %shard_map.87), calls=%async_computation.7 | async-start | bytes 655360 | tf_op jit(solution)/shard_map/all_to_all | solution.py:383
  231.6 6.7 %collective-permute-done.23.ns = f32[512,128]{1,0:T(8,128)S(1)} collective-permute-done((f32[512,128]{1,0:T(8,128)}, f32[512,128]{1,0:T(8,128)S(1)}, u32[]{:S(2)}, u32[]{:S(2)}) %collective-permute-start.23) | collective-permute-done | bytes 262176 | tf_op jit(solution)/shard_map/ppermute | solution.py:35
  238.2 2.0 collective-permute-done.24.ne
  240.3 1.2 copy-done.14
  241.5 1.2 copy-done.16
  242.7 1.0 copy-done.22
  243.8 1.0 copy-done.24
  246.7 2.0 shard_map.88
  (149 shorter events, 41.6 us)
Async XLA Ops:
  0.6 62.8 %copy-start.61 = (s32[1,1,16]{2,1,0:T(1,128)S(1)}, s32[1,1,16]{2,1,0:T(1,128)}, u32[]{:S(2)}) copy-start(s32[1,1,16]{2,1,0:T(1,128)} %param.9) | copy-start | bytes 196
  1.9 10.5 %collective-permute-start.4 = (f32[32,8,128]{2,1,0:T(8,128)S(1)}, f32[32,8,128]{2,1,0:T(8,128)S(1)}, u32[]{:S(2)}, u32[]{:S(2)}) collective-permute-start(f32[32,8,128]{2,1,0:T(8,128)S(1)} %get-tuple-element.69), channel_id=1, source_target_pairs={{0,32},{32,64},{64,96},{96,128},{128,160},{160,192},{192,224},{224... | collective-permute-start | bytes 393224 | tf_op jit(solution)/shard_map/ppermute | solution.py:35
  4.4 8.0 %collective-permute-start.5 = (f32[32,8,128]{2,1,0:T(8,128)S(1)}, f32[32,8,128]{2,1,0:T(8,128)S(1)}, u32[]{:S(2)}, u32[]{:S(2)}) collective-permute-start(f32[32,8,128]{2,1,0:T(8,128)S(1)} %get-tuple-element.69), channel_id=1, source_target_pairs={{0,224},{32,0},{64,32},{96,64},{128,96},{160,128},{192,160},{224,1... | collective-permute-start | bytes 393224 | tf_op jit(solution)/shard_map/ppermute | solution.py:35
  9.5 5.7 %collective-permute-start.10 = (f32[128,512]{1,0:T(8,128)S(1)}, f32[128,512]{1,0:T(8,128)S(1)}, u32[]{:S(2)}, u32[]{:S(2)}) collective-permute-start(f32[128,512]{1,0:T(8,128)S(1)} %get-tuple-element.66), channel_id=1, source_target_pairs={{0,1},{1,2},{2,3},{3,4},{4,5},{5,6},{6,7},{7,8},{8,9},{9,10},{10,1... | collective-permute-start | bytes 786440 | tf_op jit(solution)/shard_map/ppermute | solution.py:35
  11.7 8.6 %collective-permute-start.9 = (f32[128,512]{1,0:T(8,128)S(1)}, f32[128,512]{1,0:T(8,128)S(1)}, u32[]{:S(2)}, u32[]{:S(2)}) collective-permute-start(f32[128,512]{1,0:T(8,128)S(1)} %get-tuple-element.67), channel_id=1, source_target_pairs={{0,32},{32,64},{64,96},{96,128},{128,160},{160,192},{192,224},{224... | collective-permute-start | bytes 786440 | tf_op jit(solution)/shard_map/ppermute | solution.py:35
  12.4 17.3 %collective-permute-start.7 = (f32[3,32,8,128]{3,2,1,0:T(8,128)S(1)}, f32[3,32,8,128]{3,2,1,0:T(8,128)S(1)}, u32[]{:S(2)}, u32[]{:S(2)}) collective-permute-start(f32[3,32,8,128]{3,2,1,0:T(8,128)S(1)} %pad_maximum_fusion.mine), channel_id=1, source_target_pairs={{0,31},{1,0},{2,1},{3,2},{4,3},{5,4},{6,5},{7,6},{8,7},{9,8},{10,9... | collective-permute-start | bytes 1179656 | tf_op jit(solution)/shard_map/ppermute | solution.py:35
  12.9 16.8 %collective-permute-start.6 = (f32[3,32,8,128]{3,2,1,0:T(8,128)S(1)}, f32[3,32,8,128]{3,2,1,0:T(8,128)S(1)}, u32[]{:S(2)}, u32[]{:S(2)}) collective-permute-start(f32[3,32,8,128]{3,2,1,0:T(8,128)S(1)} %pad_maximum_fusion.mine), channel_id=1, source_target_pairs={{0,1},{1,2},{2,3},{3,4},{4,5},{5,6},{6,7},{7,8},{8,9},{9,10},{10,1... | collective-permute-start | bytes 1179656 | tf_op jit(solution)/shard_map/ppermute | solution.py:35
  20.3 1.0 copy-start.4
  23.2 1.0 copy-start.5
  24.2 15.6 %all-to-all-start = ((f32[8,48,128]{2,1,0:T(8,128)}), f32[8,48,128]{2,1,0:T(8,128)S(1)}, u32[]{:S(2)}, u32[]{:S(2)}) async-start(f32[8,48,128]{2,1,0:T(8,128)} %get-tuple-element.34), calls=%async_computation | async-start | bytes 393216 | tf_op jit(solution)/shard_map/all_to_all | solution.py:373
  29.8 11.4 %collective-permute-start.8 = (f32[3,32,8,128]{3,2,1,0:T(8,128)S(1)}, f32[3,32,8,128]{3,2,1,0:T(8,128)S(1)}, u32[]{:S(2)}, u32[]{:S(2)}) collective-permute-start(f32[3,32,8,128]{3,2,1,0:T(8,128)S(1)} %broadcast_select_fusion), channel_id=1, source_target_pairs={{0,1},{1,0},{2,3},{3,2},{4,5},{5,4},{6,7},{7,6},{8,9},{9,8},{10,11... | collective-permute-start | bytes 1179656 | tf_op jit(solution)/shard_map/ppermute | solution.py:45
  39.9 2.4 collective-permute-start.11
  43.5 19.9 %all-to-all-start.1 = ((f32[16,40,128]{2,1,0:T(8,128)}), f32[16,40,128]{2,1,0:T(8,128)S(1)}, u32[]{:S(2)}, u32[]{:S(2)}) async-start(f32[16,40,128]{2,1,0:T(8,128)} %shard_map.81), calls=%async_computation.1 | async-start | bytes 655360 | tf_op jit(solution)/shard_map/all_to_all | solution.py:383
  50.2 11.3 %collective-permute-start.3 = (f32[6,512]{1,0:T(8,128)S(1)}, f32[6,512]{1,0:T(8,128)S(1)}, u32[]{:S(2)}, u32[]{:S(2)}) collective-permute-start(f32[6,512]{1,0:T(8,128)S(1)} %get-tuple-element.70), channel_id=1, source_target_pairs={{1,0},{2,1},{3,2},{4,3},{5,4},{6,5},{7,6},{8,7},{9,8},{10,9},{11,1... | collective-permute-start | bytes 36872 | tf_op jit(solution)/shard_map/ppermute | solution.py:41
  52.8 8.8 %collective-permute-start.2 = (f32[6,512]{1,0:T(8,128)S(1)}, f32[6,512]{1,0:T(8,128)S(1)}, u32[]{:S(2)}, u32[]{:S(2)}) collective-permute-start(f32[6,512]{1,0:T(8,128)S(1)} %get-tuple-element.71), channel_id=1, source_target_pairs={{0,1},{1,2},{2,3},{3,4},{4,5},{5,6},{6,7},{7,8},{8,9},{9,10},{10,1... | collective-permute-start | bytes 36872 | tf_op jit(solution)/shard_map/ppermute | solution.py:41
  56.2 5.3 %collective-permute-start.1 = (f32[6,512]{1,0:T(8,128)S(1)}, f32[6,512]{1,0:T(8,128)S(1)}, u32[]{:S(2)}, u32[]{:S(2)}) collective-permute-start(f32[6,512]{1,0:T(8,128)S(1)} %get-tuple-element.72), channel_id=1, source_target_pairs={{32,0},{64,32},{96,64},{128,96},{160,128},{192,160},{224,192},{33,... | collective-permute-start | bytes 36872 | tf_op jit(solution)/shard_map/ppermute | solution.py:41
  57.5 4.8 %collective-permute-start = (f32[6,512]{1,0:T(8,128)S(1)}, f32[6,512]{1,0:T(8,128)S(1)}, u32[]{:S(2)}, u32[]{:S(2)}) collective-permute-start(f32[6,512]{1,0:T(8,128)S(1)} %get-tuple-element.73), channel_id=1, source_target_pairs={{0,32},{32,64},{64,96},{96,128},{128,160},{160,192},{192,224},{1,3... | collective-permute-start | bytes 36872 | tf_op jit(solution)/shard_map/ppermute | solution.py:41
  63.4 3.4 %copy-start.3 = (bf16[1,1,2048,2048]{3,2,1,0:T(8,128)(2,1)S(1)}, bf16[1,1,2048,2048]{3,2,1,0:T(8,128)(2,1)}, u32[]{:S(2)}) copy-start(bf16[1,1,2048,2048]{3,2,1,0:T(8,128)(2,1)} %param.6) | copy-start | bytes 25165828
  66.8 1.2 copy-start.6
  75.2 3.3 %copy-start = (bf16[2048,2048]{1,0:T(8,128)(2,1)}, bf16[2048,2048]{1,0:T(8,128)(2,1)S(1)}, u32[]{:S(2)}) copy-start(bf16[2048,2048]{1,0:T(8,128)(2,1)S(1)} %get-tuple-element.36.refs_2_) | copy-start | bytes 25165828
  78.5 1.0 copy-start.17
  81.6 17.7 %copy-start.41 = (f32[512,128]{1,0:T(8,128)}, f32[512,128]{1,0:T(8,128)S(1)}, u32[]{:S(2)}) copy-start(f32[512,128]{1,0:T(8,128)S(1)} %get-tuple-element.40.refs_11_) | copy-start | bytes 786436
  96.3 3.1 %collective-permute-start.12 = (f32[8,48,128]{2,1,0:T(8,128)S(1)}, f32[8,48,128]{2,1,0:T(8,128)S(1)}, u32[]{:S(2)}, u32[]{:S(2)}) collective-permute-start(f32[8,48,128]{2,1,0:T(8,128)S(1)} %all_to_all.40.own), channel_id=1, source_target_pairs={{0,1},{1,0},{2,3},{3,2},{4,5},{5,4},{6,7},{7,6},{8,9},{9,8},{10,11... | collective-permute-start | bytes 589832 | tf_op jit(solution)/shard_map/ppermute | solution.py:45
  100.6 20.1 %all-to-all-start.3 = ((f32[16,40,128]{2,1,0:T(8,128)}), f32[16,40,128]{2,1,0:T(8,128)S(1)}, u32[]{:S(2)}, u32[]{:S(2)}) async-start(f32[16,40,128]{2,1,0:T(8,128)} %shard_map.83), calls=%async_computation.3 | async-start | bytes 655360 | tf_op jit(solution)/shard_map/all_to_all | solution.py:383
  108.3 8.7 %collective-permute-start.13 = (f32[512,128]{1,0:T(8,128)}, f32[512,128]{1,0:T(8,128)S(1)}, u32[]{:S(2)}, u32[]{:S(2)}) collective-permute-start(f32[512,128]{1,0:T(8,128)} %copy-done.43), channel_id=1, source_target_pairs={{0,32},{32,64},{64,96},{96,128},{128,160},{160,192},{192,224},{224... | collective-permute-start | bytes 786440 | tf_op jit(solution)/shard_map/ppermute | solution.py:35
  108.5 9.3 %collective-permute-start.14 = (f32[512,128]{1,0:T(8,128)}, f32[512,128]{1,0:T(8,128)S(1)}, u32[]{:S(2)}, u32[]{:S(2)}) collective-permute-start(f32[512,128]{1,0:T(8,128)} %copy-done.41), channel_id=1, source_target_pairs={{0,224},{32,0},{64,32},{96,64},{128,96},{160,128},{192,160},{224,1... | collective-permute-start | bytes 786440 | tf_op jit(solution)/shard_map/ppermute | solution.py:35
  111.1 7.4 %collective-permute-start.15 = (f32[512,128]{1,0:T(8,128)}, f32[512,128]{1,0:T(8,128)S(1)}, u32[]{:S(2)}, u32[]{:S(2)}) collective-permute-start(f32[512,128]{1,0:T(8,128)} %copy-done.47), channel_id=1, source_target_pairs={{0,1},{1,2},{2,3},{3,4},{4,5},{5,6},{6,7},{7,8},{8,9},{9,10},{10,1... | collective-permute-start | bytes 786440 | tf_op jit(solution)/shard_map/ppermute | solution.py:35
  113.8 6.3 %collective-permute-start.16 = (f32[512,128]{1,0:T(8,128)}, f32[512,128]{1,0:T(8,128)S(1)}, u32[]{:S(2)}, u32[]{:S(2)}) collective-permute-start(f32[512,128]{1,0:T(8,128)} %copy-done.45), channel_id=1, source_target_pairs={{0,31},{1,0},{2,1},{3,2},{4,3},{5,4},{6,5},{7,6},{8,7},{9,8},{10,9... | collective-permute-start | bytes 786440 | tf_op jit(solution)/shard_map/ppermute | solution.py:35
  120.8 3.4 %copy-start.1 = (bf16[2048,2048]{1,0:T(8,128)(2,1)S(1)}, bf16[2048,2048]{1,0:T(8,128)(2,1)}, u32[]{:S(2)}) copy-start(bf16[2048,2048]{1,0:T(8,128)(2,1)} %copy-done) | copy-start | bytes 25165828
  124.2 1.2 copy-start.18
  125.4 0.9 copy-start.42
  126.3 0.9 copy-start.44
  127.3 0.9 copy-start.46
  128.2 0.9 copy-start.48
  129.2 0.9 copy-start.54
  130.1 0.9 copy-start.56
  131.1 0.9 copy-start.58
  132.0 0.9 copy-start.60
  137.6 1.0 copy-start.7
  138.6 1.0 copy-start.9
  139.6 1.0 copy-start.11
  143.5 15.5 %copy-start.25 = (f32[512,128]{1,0:T(8,128)}, f32[512,128]{1,0:T(8,128)S(1)}, u32[]{:S(2)}) copy-start(f32[512,128]{1,0:T(8,128)S(1)} %get-tuple-element.46.refs_11_) | copy-start | bytes 786436
  154.6 4.5 %collective-permute-start.17 = (f32[8,48,128]{2,1,0:T(8,128)S(1)}, f32[8,48,128]{2,1,0:T(8,128)S(1)}, u32[]{:S(2)}, u32[]{:S(2)}) collective-permute-start(f32[8,48,128]{2,1,0:T(8,128)S(1)} %all_to_all.41.own), channel_id=1, source_target_pairs={{0,1},{1,0},{2,3},{3,2},{4,5},{5,4},{6,7},{7,6},{8,9},{9,8},{10,11... | collective-permute-start | bytes 589832 | tf_op jit(solution)/shard_map/ppermute | solution.py:45
  160.3 19.5 %all-to-all-start.5 = ((f32[16,40,128]{2,1,0:T(8,128)}), f32[16,40,128]{2,1,0:T(8,128)S(1)}, u32[]{:S(2)}, u32[]{:S(2)}) async-start(f32[16,40,128]{2,1,0:T(8,128)} %shard_map.85), calls=%async_computation.5 | async-start | bytes 655360 | tf_op jit(solution)/shard_map/all_to_all | solution.py:383
  167.4 8.7 %collective-permute-start.18 = (f32[512,128]{1,0:T(8,128)}, f32[512,128]{1,0:T(8,128)S(1)}, u32[]{:S(2)}, u32[]{:S(2)}) collective-permute-start(f32[512,128]{1,0:T(8,128)} %copy-done.27), channel_id=1, source_target_pairs={{0,32},{32,64},{64,96},{96,128},{128,160},{160,192},{192,224},{224... | collective-permute-start | bytes 786440 | tf_op jit(solution)/shard_map/ppermute | solution.py:35
  167.8 9.1 %collective-permute-start.19 = (f32[512,128]{1,0:T(8,128)}, f32[512,128]{1,0:T(8,128)S(1)}, u32[]{:S(2)}, u32[]{:S(2)}) collective-permute-start(f32[512,128]{1,0:T(8,128)} %copy-done.25), channel_id=1, source_target_pairs={{0,224},{32,0},{64,32},{96,64},{128,96},{160,128},{192,160},{224,1... | collective-permute-start | bytes 786440 | tf_op jit(solution)/shard_map/ppermute | solution.py:35
  170.1 7.4 %collective-permute-start.20 = (f32[512,128]{1,0:T(8,128)}, f32[512,128]{1,0:T(8,128)S(1)}, u32[]{:S(2)}, u32[]{:S(2)}) collective-permute-start(f32[512,128]{1,0:T(8,128)} %copy-done.31), channel_id=1, source_target_pairs={{0,1},{1,2},{2,3},{3,4},{4,5},{5,6},{6,7},{7,8},{8,9},{9,10},{10,1... | collective-permute-start | bytes 786440 | tf_op jit(solution)/shard_map/ppermute | solution.py:35
  172.8 6.3 %collective-permute-start.21 = (f32[512,128]{1,0:T(8,128)}, f32[512,128]{1,0:T(8,128)S(1)}, u32[]{:S(2)}, u32[]{:S(2)}) collective-permute-start(f32[512,128]{1,0:T(8,128)} %copy-done.29), channel_id=1, source_target_pairs={{0,31},{1,0},{2,1},{3,2},{4,3},{5,4},{6,5},{7,6},{8,7},{9,8},{10,9... | collective-permute-start | bytes 786440 | tf_op jit(solution)/shard_map/ppermute | solution.py:35
  179.8 3.4 %copy-start.2 = (bf16[2048,2048]{1,0:T(8,128)(2,1)S(1)}, bf16[2048,2048]{1,0:T(8,128)(2,1)}, u32[]{:S(2)}) copy-start(bf16[2048,2048]{1,0:T(8,128)(2,1)} %copy-done) | copy-start | bytes 25165828
  183.2 1.2 copy-start.8
  184.4 1.2 copy-start.10
  185.7 1.2 copy-start.12
  186.9 1.0 copy-start.20
  201.2 1.0 copy-start.13
  202.2 1.0 copy-start.15
  206.9 15.5 %copy-start.49 = (f32[512,128]{1,0:T(8,128)}, f32[512,128]{1,0:T(8,128)S(1)}, u32[]{:S(2)}) copy-start(f32[512,128]{1,0:T(8,128)S(1)} %get-tuple-element.58.ys) | copy-start | bytes 786436
  217.9 4.5 %collective-permute-start.22 = (f32[8,48,128]{2,1,0:T(8,128)S(1)}, f32[8,48,128]{2,1,0:T(8,128)S(1)}, u32[]{:S(2)}, u32[]{:S(2)}) collective-permute-start(f32[8,48,128]{2,1,0:T(8,128)S(1)} %all_to_all.42.own), channel_id=1, source_target_pairs={{0,1},{1,0},{2,3},{3,2},{4,5},{5,4},{6,7},{7,6},{8,9},{9,8},{10,11... | collective-permute-start | bytes 589832 | tf_op jit(solution)/shard_map/ppermute | solution.py:45
  223.7 16.6 %all-to-all-start.7 = ((f32[16,40,128]{2,1,0:T(8,128)}), f32[16,40,128]{2,1,0:T(8,128)S(1)}, u32[]{:S(2)}, u32[]{:S(2)}) async-start(f32[16,40,128]{2,1,0:T(8,128)} %shard_map.87), calls=%async_computation.7 | async-start | bytes 655360 | tf_op jit(solution)/shard_map/all_to_all | solution.py:383
  230.7 7.5 %collective-permute-start.23 = (f32[512,128]{1,0:T(8,128)}, f32[512,128]{1,0:T(8,128)S(1)}, u32[]{:S(2)}, u32[]{:S(2)}) collective-permute-start(f32[512,128]{1,0:T(8,128)} %copy-done.63), channel_id=1, source_target_pairs={{0,224},{32,0},{64,32},{96,64},{128,96},{160,128},{192,160},{224,1... | collective-permute-start | bytes 786440 | tf_op jit(solution)/shard_map/ppermute | solution.py:35
  230.8 9.4 %collective-permute-start.24 = (f32[512,128]{1,0:T(8,128)}, f32[512,128]{1,0:T(8,128)S(1)}, u32[]{:S(2)}, u32[]{:S(2)}) collective-permute-start(f32[512,128]{1,0:T(8,128)} %copy-done.62), channel_id=1, source_target_pairs={{0,31},{1,0},{2,1},{3,2},{4,3},{5,4},{6,5},{7,6},{8,7},{9,8},{10,9... | collective-permute-start | bytes 786440 | tf_op jit(solution)/shard_map/ppermute | solution.py:35
  240.3 1.2 copy-start.14
  241.5 1.2 copy-start.16
  242.7 1.0 copy-start.22
  243.8 1.0 copy-start.24
  (30 other events, 23.9 us)
